TPU v7x, 512 devices: a whole 4x8x8 slice. The times are simulated.
512 devices in a mesh: lat: 64 (over y, z_hi, core), lon: 8 (over x, z_lo).
Axes of the slice: x: 4, y: 8, z: 8 (z_hi: 4, z_lo: 2; z = z_hi * 2 + z_lo), core: 2. Of those that a mesh axis runs over, the one named last changes fastest.
Arguments:
- tracers: float32 [16, 6, 256, 2048], P(None, None, 'lat', 'lon'), may hold values from -6 to 6
- velocity: float32 [2, 256, 2048], P(None, 'lat', 'lon'), may hold values from -4 to 4
- stress: float32 [3, 256, 2048], P(None, 'lat', 'lon'), may hold values from -6 to 6
- strength: float32 [256, 2048], P('lat', 'lon'), may hold values from 0.5 to 5
- inverse_mass: float32 [256, 2048], P('lat', 'lon'), may hold values from 0.2 to 2
- wind: float32 [2, 256, 2048], P(None, 'lat', 'lon'), may hold values from -4 to 4
- ocean_mask: int32 [256, 2048], P('lat', 'lon'), may hold values 0 or 1
Outputs:
- new_velocity: float32 [2, 256, 2048], P(None, 'lat', 'lon')
- new_stress: float32 [3, 256, 2048], P(None, 'lat', 'lon')
- new_tracers: float32 [16, 6, 256, 2048], P(None, None, 'lat', 'lon')
All inputs are finite; a program needn't handle non-finite values. No bound on the sum of `ocean_mask` on one device may be relied on, other than what follows from the above.
Results may differ from a plain program's by a relative error of at most 0.00007.
Values sent between devices are 32-bit elements; how exact they have to be, the bound alone decides.
A program may use at most 64 MiB of HBM per device.

v0:
```python
import math

import jax
import jax.numpy as jnp
import numpy as np
from jax import lax
from jax.sharding import PartitionSpec as P

ITERS = 2


ellipse_inv = 0.25
floor_rate = 0.1
relax_stress = 3.0
relax_velocity = 3.0
drag_rate = 1.0
time_step = 0.15


def shifted(x, axis, by):
    size = lax.axis_size(axis)
    pairs = [(i, i + by) for i in range(size) if 0 <= i + by < size]
    return lax.ppermute(x, axis, pairs)


def passed_along(value, axis, steps):
    count = lax.axis_size(axis)
    pairs = [(source, (source + steps) % count) for source in range(count)]
    return lax.ppermute(value, axis, pairs)


def with_halo(cells, sides, width):
    for axis, dim in sides:
        count = lax.axis_size(axis)
        head = lax.slice_in_dim(cells, 0, width, axis=dim)
        tail = lax.slice_in_dim(cells, cells.shape[dim] - width, cells.shape[dim], axis=dim)
        cells = jnp.concatenate(
            [
                lax.ppermute(tail, axis, [(i, (i + 1) % count) for i in range(count)]),
                cells,
                lax.ppermute(head, axis, [((i + 1) % count, i) for i in range(count)]),
            ],
            axis=dim,
        )
    return cells


def basis_values(xi, eta):
    return [1.0, xi, eta, 1.5 * xi * xi - 0.5, xi * eta, 1.5 * eta * eta - 0.5]


def quad_tables():
    root = math.sqrt(0.6)
    gauss = [-root, 0.0, root]
    weights = [5.0 / 9.0, 8.0 / 9.0, 5.0 / 9.0]
    points = [(gauss[a], gauss[b], weights[a] * weights[b]) for b in range(3) for a in range(3)]
    volume = np.array([basis_values(x, e) for x, e, w in points])
    slope_xi = np.array([[0.0, w, 0.0, 3.0 * x * w, e * w, 0.0] for x, e, w in points])
    slope_eta = np.array([[0.0, 0.0, w, 0.0, x * w, 3.0 * e * w] for x, e, w in points])
    shape = np.array(
        [
            [
                (1 - x) * (1 - e) / 4,
                (1 + x) * (1 - e) / 4,
                (1 - x) * (1 + e) / 4,
                (1 + x) * (1 + e) / 4,
            ]
            for x, e, w in points
        ]
    )
    north = np.array([basis_values(s, 1.0) for s in gauss])
    south = np.array([basis_values(s, -1.0) for s in gauss])
    east = np.array([basis_values(1.0, s) for s in gauss])
    west = np.array([basis_values(-1.0, s) for s in gauss])
    wcol = np.array(weights)[:, None]
    gcol = np.array(gauss)
    return {
        "volume": volume,
        "slope_xi": slope_xi,
        "slope_eta": slope_eta,
        "shape": shape,
        "faces": np.concatenate([north, south, east, west], 0),
        "north_w": wcol * north,
        "south_w": wcol * south,
        "east_w": wcol * east,
        "west_w": wcol * west,
        "half_low": (1 - gcol) / 2,
        "half_high": (1 + gcol) / 2,
        "inv_mass": 1.0 / np.array([4.0, 4.0 / 3.0, 4.0 / 3.0, 0.8, 4.0 / 9.0, 0.8]),
    }


def table(tabs, name):
    return jnp.asarray(tabs[name], jnp.float32)


def contract(form, left, right):
    return jnp.einsum(form, left, right, precision=lax.Precision.HIGHEST)


def face_traces(coefs, tabs):
    every = contract("fk,rkxy->rfxy", table(tabs, "faces"), coefs)
    return (every[:, 0:3], every[:, 3:6], every[:, 6:9], every[:, 9:12])


def dg_rate(coefs, traces, ocean, uext, rims, row_factor, tabs):
    north, south, east, west = traces
    (
        low_row,
        low_row_mask,
        high_row,
        high_row_mask,
        low_col,
        low_col_mask,
        high_col,
        high_col_mask,
    ) = rims
    half_low = table(tabs, "half_low")[:, None, None]
    half_high = table(tabs, "half_high")[:, None, None]
    lower = jnp.concatenate([low_row[:, :, None, :], north], 2)
    upper = jnp.concatenate([south, high_row[:, :, None, :]], 2)
    row_active = (
        jnp.concatenate([low_row_mask[None], ocean], 0)
        * jnp.concatenate([ocean, high_row_mask[None]], 0)
        * row_factor[:, None]
    )
    normal_row = half_low * uext[1][None, :, :-1] + half_high * uext[1][None, :, 1:]
    row_flux = (
        jnp.maximum(normal_row, 0.0) * lower + jnp.minimum(normal_row, 0.0) * upper
    ) * row_active
    row_part = contract("sm,rsxy->rmxy", table(tabs, "south_w"), row_flux[:, :, :-1]) - contract(
        "sm,rsxy->rmxy", table(tabs, "north_w"), row_flux[:, :, 1:]
    )
    left = jnp.concatenate([low_col[:, :, :, None], east], 3)
    right = jnp.concatenate([west, high_col[:, :, :, None]], 3)
    col_active = jnp.concatenate([low_col_mask[:, None], ocean], 1) * jnp.concatenate(
        [ocean, high_col_mask[:, None]], 1
    )
    normal_col = half_low * uext[0][None, :-1, :] + half_high * uext[0][None, 1:, :]
    col_flux = (
        jnp.maximum(normal_col, 0.0) * left + jnp.minimum(normal_col, 0.0) * right
    ) * col_active
    col_part = contract("sm,rsxy->rmxy", table(tabs, "west_w"), col_flux[..., :-1]) - contract(
        "sm,rsxy->rmxy", table(tabs, "east_w"), col_flux[..., 1:]
    )
    corners = jnp.stack([uext[:, :-1, :-1], uext[:, :-1, 1:], uext[:, 1:, :-1], uext[:, 1:, 1:]], 1)
    at_points = contract("pa,caxy->cpxy", table(tabs, "shape"), corners)
    values = contract("pk,rkxy->rpxy", table(tabs, "volume"), coefs)
    volume = contract("pm,rpxy->rmxy", table(tabs, "slope_xi"), values * at_points[0]) + contract(
        "pm,rpxy->rmxy", table(tabs, "slope_eta"), values * at_points[1]
    )
    return (volume + row_part + col_part) * table(tabs, "inv_mass")[None, :, None, None] * ocean


def stress_forces(current, uext, strength, ocean):
    c00 = uext[:, :-1, :-1]
    c10 = uext[:, :-1, 1:]
    c01 = uext[:, 1:, :-1]
    c11 = uext[:, 1:, 1:]
    along_x = 0.5 * (c10 + c11 - c00 - c01)
    along_y = 0.5 * (c01 + c11 - c00 - c10)
    strain_xx = along_x[0]
    strain_yy = along_y[1]
    strain_xy = 0.5 * (along_y[0] + along_x[1])
    delta = jnp.sqrt(
        (strain_xx * strain_xx + strain_yy * strain_yy) * (1.0 + ellipse_inv)
        + 4.0 * ellipse_inv * strain_xy * strain_xy
        + 2.0 * strain_xx * strain_yy * (1.0 - ellipse_inv)
        + floor_rate * floor_rate
    )
    zeta = strength / (2.0 * delta)
    shear = zeta * ellipse_inv
    trace_rate = strain_xx + strain_yy
    plastic = jnp.stack(
        [
            2.0 * shear * strain_xx + (zeta - shear) * trace_rate - 0.5 * strength,
            2.0 * shear * strain_yy + (zeta - shear) * trace_rate - 0.5 * strength,
            2.0 * shear * strain_xy,
        ],
        0,
    )
    current = ocean * (current + (plastic - current) / relax_stress)
    forces = []
    for sign_x, sign_y in ((-1.0, -1.0), (1.0, -1.0), (-1.0, 1.0), (1.0, 1.0)):
        force_x = -0.5 * (current[0] * sign_x + current[2] * sign_y)
        force_y = -0.5 * (current[2] * sign_x + current[1] * sign_y)
        forces.append(jnp.stack([force_x, force_y], 0))
    return (current, jnp.stack(forces, 1))


def spread_corners(terms):
    return (
        jnp.pad(terms[:, 0], ((0, 0), (0, 1), (0, 1)))
        + jnp.pad(terms[:, 1], ((0, 0), (0, 1), (1, 0)))
        + jnp.pad(terms[:, 2], ((0, 0), (1, 0), (0, 1)))
        + jnp.pad(terms[:, 3], ((0, 0), (1, 0), (1, 0)))
    )


def update_velocity(moving, velocity, inverse_mass, force, wind, active):
    return (
        active
        * (relax_velocity * moving + velocity + inverse_mass * (force + wind))
        / (1.0 + relax_velocity + inverse_mass * drag_rate)
    )


def node_corners(moving):
    top = shifted(moving[:, 0:1, :], "lat", -1)
    extended = jnp.concatenate([moving, top], 1)
    side = passed_along(extended[:, :, 0:1], "lon", -1)
    return jnp.concatenate([extended, side], 2)


def assemble(terms):
    grid = spread_corners(terms)
    width = grid.shape[2] - 1
    height = grid.shape[1] - 1
    column = passed_along(grid[:, :, width], "lon", 1)
    folded = jnp.concatenate([grid[:, :, 0:1] + column[:, :, None], grid[:, :, 1:width]], 2)
    row = shifted(folded[:, height, :], "lat", 1)
    return jnp.concatenate([folded[:, 0:1, :] + row[:, None, :], folded[:, 1:height, :]], 1)


def local(tracers, velocity, stress, strength, inverse_mass, wind, ocean_mask):
    tabs = quad_tables()
    rows_here = ocean_mask.shape[0]
    cols_here = ocean_mask.shape[1]
    count_tr = tracers.shape[0]
    band = lax.axis_index("lat")
    bands = lax.axis_size("lat")
    first_band = (band > 0).astype(jnp.float32)
    last_band = (band < bands - 1).astype(jnp.float32)
    ocean = ocean_mask.astype(jnp.float32)
    count = assemble(jnp.broadcast_to(ocean, (1, 4) + ocean.shape))
    row_mask = jnp.concatenate([first_band[None], jnp.ones((rows_here - 1,), jnp.float32)], 0)[
        :, None
    ]
    active = jnp.minimum(count[0], 1.0) * row_mask
    moving = velocity
    current = stress
    for turn in range(ITERS):
        current, forces = stress_forces(current, node_corners(moving), strength, ocean)
        moving = update_velocity(moving, velocity, inverse_mass, assemble(forces), wind, active)
    split = count_tr * 6
    uext = node_corners(moving)
    row_factor = jnp.concatenate(
        [first_band[None], jnp.ones((rows_here - 1,), jnp.float32), last_band[None]], 0
    )

    def rate(coefs):
        traces = face_traces(coefs, tabs)
        stacked = jnp.concatenate([coefs.reshape(split, rows_here, cols_here), ocean[None]], 0)
        ext = with_halo(stacked, (("lat", 1), ("lon", 2)), 1)
        faces = table(tabs, "faces")
        south_row = ext[:split, 0, 1:-1].reshape(count_tr, 6, cols_here)
        north_row = ext[:split, rows_here + 1, 1:-1].reshape(count_tr, 6, cols_here)
        west_col = ext[:split, 1:-1, 0].reshape(count_tr, 6, rows_here)
        east_col = ext[:split, 1:-1, cols_here + 1].reshape(count_tr, 6, rows_here)
        rims = (
            contract("sk,rky->rsy", faces[0:3], south_row),
            ext[split, 0, 1:-1],
            contract("sk,rky->rsy", faces[3:6], north_row),
            ext[split, rows_here + 1, 1:-1],
            contract("sk,rky->rsy", faces[6:9], west_col),
            ext[split, 1:-1, 0],
            contract("sk,rky->rsy", faces[9:12], east_col),
            ext[split, 1:-1, cols_here + 1],
        )
        return dg_rate(coefs, traces, ocean, uext, rims, row_factor, tabs)

    first = tracers + time_step * rate(tracers)
    second = 0.75 * tracers + 0.25 * (first + time_step * rate(first))
    third = tracers / 3.0 + 2.0 / 3.0 * (second + time_step * rate(second))
    return (moving, current, ocean * third)


def solution(mesh):
    in_specs = (
        P(None, None, "lat", "lon"),
        P(None, "lat", "lon"),
        P(None, "lat", "lon"),
        P("lat", "lon"),
        P("lat", "lon"),
        P(None, "lat", "lon"),
        P("lat", "lon"),
    )
    out_specs = (P(None, "lat", "lon"), P(None, "lat", "lon"), P(None, None, "lat", "lon"))
    return jax.shard_map(local, mesh=mesh, in_specs=in_specs, out_specs=out_specs, check_vma=False)
```

profile of v0, /device:TPU:34, one launch (start us, length us, event | category | flops | bytes accessed | tf_op | source)
XLA Modules:
  0.0 219.8 jit_solution(1691542425704980453)
XLA Ops:
  1.4 10.3 %collective-permute-start.2 = (f32[2,1,256]{2,1,0:T(1,128)S(1)}, f32[2,1,256]{2,1,0:T(1,128)S(1)}, u32[]{:S(2)}, u32[]{:S(2)}) collective-permute-start(f32[2,1,256]{2,1,0:T(1,128)S(1)} %slice.455), channel_id=1, source_target_pairs={{8,0},{16,8},{24,16},{32,24},{40,32},{48,40},{56,48},{64,56},{72,6... | collective-permute-start | bytes 6152 | tf_op jit(solution)/shard_map/ppermute | solution.py:23
  11.9 3.4 %collective-permute-start = (f32[1,5]{1,0:T(1,128)S(1)}, f32[1,5]{1,0:T(1,128)S(1)}, u32[]{:S(2)}, u32[]{:S(2)}) collective-permute-start(f32[1,5]{1,0:T(1,128)S(1)} %bitcast.344), channel_id=1, source_target_pairs={{0,1},{1,2},{2,3},{3,4},{4,5},{5,6},{6,7},{7,0},{8,9},{9,10},{10,1... | collective-permute-start | bytes 68 | tf_op jit(solution)/shard_map/ppermute | solution.py:29
  15.3 2.1 fusion.72
  19.3 7.9 %collective-permute-start.13 = (f32[97,1,256]{2,1,0:T(1,128)}, f32[97,1,256]{2,1,0:T(1,128)}, u32[]{:S(2)}, u32[]{:S(2)}) collective-permute-start(f32[97,1,256]{2,1,0:T(1,128)} %get-tuple-element.56), channel_id=1, source_target_pairs={{8,0},{16,8},{24,16},{32,24},{40,32},{48,40},{56,48},{64,56},{72,6... | collective-permute-start | bytes 297992 | tf_op jit(solution)/shard_map/ppermute | solution.py:41
  32.9 7.1 %collective-permute-done.1 = f32[1,256]{1,0:T(1,128)S(1)} collective-permute-done((f32[1,256]{1,0:T(1,128)S(1)}, f32[1,256]{1,0:T(1,128)S(1)}, u32[]{:S(2)}, u32[]{:S(2)}) %collective-permute-start.1) | collective-permute-done | bytes 1056 | tf_op jit(solution)/shard_map/ppermute | solution.py:23
  40.1 3.4 %collective-permute-start.3 = (f32[2,5,1]{2,1,0:T(8,128)S(1)}, f32[2,5,1]{2,1,0:T(8,128)S(1)}, u32[]{:S(2)}, u32[]{:S(2)}) collective-permute-start(f32[2,5,1]{2,1,0:T(8,128)S(1)} %fusion.113), channel_id=1, source_target_pairs={{0,7},{1,0},{2,1},{3,2},{4,3},{5,4},{6,5},{7,6},{8,15},{9,8},{10,9... | collective-permute-start | bytes 128 | tf_op jit(solution)/shard_map/ppermute | solution.py:29
  43.4 2.2 collective-permute-done.3
  47.3 4.3 %collective-permute-start.4 = (f32[2,5]{1,0:T(2,128)S(1)}, f32[2,5]{1,0:T(2,128)S(1)}, u32[]{:S(2)}, u32[]{:S(2)}) collective-permute-start(f32[2,5]{1,0:T(2,128)S(1)} %slice_reduce_fusion.9), channel_id=1, source_target_pairs={{0,1},{1,2},{2,3},{3,4},{4,5},{5,6},{6,7},{7,0},{8,9},{9,10},{10,1... | collective-permute-start | bytes 128 | tf_op jit(solution)/shard_map/ppermute | solution.py:29
  51.6 2.1 collective-permute-done.4
  55.9 7.1 %collective-permute-done.5 = f32[2,256]{1,0:T(2,128)S(1)} collective-permute-done((f32[2,256]{1,0:T(2,128)S(1)}, f32[2,256]{1,0:T(2,128)S(1)}, u32[]{:S(2)}, u32[]{:S(2)}) %collective-permute-start.5) | collective-permute-done | bytes 2080 | tf_op jit(solution)/shard_map/ppermute | solution.py:23
  66.3 3.3 %collective-permute-start.7 = (f32[2,5,1]{2,1,0:T(8,128)S(1)}, f32[2,5,1]{2,1,0:T(8,128)S(1)}, u32[]{:S(2)}, u32[]{:S(2)}) collective-permute-start(f32[2,5,1]{2,1,0:T(8,128)S(1)} %fusion.112), channel_id=1, source_target_pairs={{0,7},{1,0},{2,1},{3,2},{4,3},{5,4},{6,5},{7,6},{8,15},{9,8},{10,9... | collective-permute-start | bytes 128 | tf_op jit(solution)/shard_map/ppermute | solution.py:29
  69.7 2.2 collective-permute-done.7
  72.9 4.3 %collective-permute-start.8 = (f32[2,5]{1,0:T(2,128)S(1)}, f32[2,5]{1,0:T(2,128)S(1)}, u32[]{:S(2)}, u32[]{:S(2)}) collective-permute-start(f32[2,5]{1,0:T(2,128)S(1)} %slice_reduce_fusion.8), channel_id=1, source_target_pairs={{0,1},{1,2},{2,3},{3,4},{4,5},{5,6},{6,7},{7,0},{8,9},{9,10},{10,1... | collective-permute-start | bytes 128 | tf_op jit(solution)/shard_map/ppermute | solution.py:29
  77.2 2.1 collective-permute-done.8
  81.4 7.1 %collective-permute-done.9 = f32[2,256]{1,0:T(2,128)S(1)} collective-permute-done((f32[2,256]{1,0:T(2,128)S(1)}, f32[2,256]{1,0:T(2,128)S(1)}, u32[]{:S(2)}, u32[]{:S(2)}) %collective-permute-start.9) | collective-permute-done | bytes 2080 | tf_op jit(solution)/shard_map/ppermute | solution.py:23
  88.7 1.9 collective-permute-start.10
  91.9 3.3 %collective-permute-start.11 = (f32[2,5,1]{2,1,0:T(8,128)S(1)}, f32[2,5,1]{2,1,0:T(8,128)S(1)}, u32[]{:S(2)}, u32[]{:S(2)}) collective-permute-start(f32[2,5,1]{2,1,0:T(8,128)S(1)} %fusion.111), channel_id=1, source_target_pairs={{0,7},{1,0},{2,1},{3,2},{4,3},{5,4},{6,5},{7,6},{8,15},{9,8},{10,9... | collective-permute-start | bytes 128 | tf_op jit(solution)/shard_map/ppermute | solution.py:29
  95.3 2.1 collective-permute-done.11
  105.1 4.4 %collective-permute-start.14 = (f32[97,6,1]{2,0,1:T(8,128)S(1)}, f32[97,6,1]{2,0,1:T(8,128)S(1)}, u32[]{:S(2)}, u32[]{:S(2)}) collective-permute-start(f32[97,6,1]{2,0,1:T(8,128)S(1)} %get-tuple-element.51), channel_id=1, source_target_pairs={{0,1},{1,2},{2,3},{3,4},{4,5},{5,6},{6,7},{7,0},{8,9},{9,10},{10,1... | collective-permute-start | bytes 6992 | tf_op jit(solution)/shard_map/ppermute | solution.py:39
  109.5 2.6 %collective-permute-start.15 = (f32[97,6,1]{2,0,1:T(8,128)S(1)}, f32[97,6,1]{2,0,1:T(8,128)}, u32[]{:S(2)}, u32[]{:S(2)}) collective-permute-start(f32[97,6,1]{2,0,1:T(8,128)S(1)} %get-tuple-element.50), channel_id=1, source_target_pairs={{1,0},{2,1},{3,2},{4,3},{5,4},{6,5},{7,6},{0,7},{9,8},{10,9},{11,1... | collective-permute-start | bytes 6992 | tf_op jit(solution)/shard_map/ppermute | solution.py:41
  115.6 2.9 %collective-permute-done.14 = f32[97,6,1]{2,0,1:T(8,128)S(1)} collective-permute-done((f32[97,6,1]{2,0,1:T(8,128)S(1)}, f32[97,6,1]{2,0,1:T(8,128)S(1)}, u32[]{:S(2)}, u32[]{:S(2)}) %collective-permute-start.14) | collective-permute-done | bytes 2360 | tf_op jit(solution)/shard_map/ppermute | solution.py:39
  120.6 2.7 %collective-permute-done.15 = f32[97,6,1]{2,0,1:T(8,128)} collective-permute-done((f32[97,6,1]{2,0,1:T(8,128)S(1)}, f32[97,6,1]{2,0,1:T(8,128)}, u32[]{:S(2)}, u32[]{:S(2)}) %collective-permute-start.15) | collective-permute-done | bytes 2360 | tf_op jit(solution)/shard_map/ppermute | solution.py:41
  136.2 7.9 %collective-permute-start.17 = (f32[97,1,256]{2,1,0:T(1,128)}, f32[97,1,256]{2,1,0:T(1,128)S(1)}, u32[]{:S(2)}, u32[]{:S(2)}) collective-permute-start(f32[97,1,256]{2,1,0:T(1,128)} %get-tuple-element.54), channel_id=1, source_target_pairs={{8,0},{16,8},{24,16},{32,24},{40,32},{48,40},{56,48},{64,56},{72,6... | collective-permute-start | bytes 297992 | tf_op jit(solution)/shard_map/ppermute | solution.py:41
  149.0 4.1 %collective-permute-start.18 = (f32[97,6,1]{2,1,0:T(8,128)S(1)}, f32[97,6,1]{2,1,0:T(8,128)S(1)}, u32[]{:S(2)}, u32[]{:S(2)}) collective-permute-start(f32[97,6,1]{2,1,0:T(8,128)S(1)} %get-tuple-element.49), channel_id=1, source_target_pairs={{0,1},{1,2},{2,3},{3,4},{4,5},{5,6},{6,7},{7,0},{8,9},{9,10},{10,1... | collective-permute-start | bytes 6992 | tf_op jit(solution)/shard_map/ppermute | solution.py:39
  153.1 3.0 %collective-permute-start.19 = (f32[97,6,1]{2,1,0:T(8,128)}, f32[97,6,1]{2,1,0:T(8,128)}, u32[]{:S(2)}, u32[]{:S(2)}) collective-permute-start(f32[97,6,1]{2,1,0:T(8,128)} %get-tuple-element.48), channel_id=1, source_target_pairs={{1,0},{2,1},{3,2},{4,3},{5,4},{6,5},{7,6},{0,7},{9,8},{10,9},{11,1... | collective-permute-start | bytes 6992 | tf_op jit(solution)/shard_map/ppermute | solution.py:41
  158.3 3.6 %collective-permute-done.18 = f32[97,6,1]{2,1,0:T(8,128)S(1)} collective-permute-done((f32[97,6,1]{2,1,0:T(8,128)S(1)}, f32[97,6,1]{2,1,0:T(8,128)S(1)}, u32[]{:S(2)}, u32[]{:S(2)}) %collective-permute-start.18) | collective-permute-done | bytes 2360 | tf_op jit(solution)/shard_map/ppermute | solution.py:39
  164.0 3.4 %collective-permute-done.19 = f32[97,6,1]{2,1,0:T(8,128)} collective-permute-done((f32[97,6,1]{2,1,0:T(8,128)}, f32[97,6,1]{2,1,0:T(8,128)}, u32[]{:S(2)}, u32[]{:S(2)}) %collective-permute-start.19) | collective-permute-done | bytes 2360 | tf_op jit(solution)/shard_map/ppermute | solution.py:41
  180.0 7.9 %collective-permute-start.21 = (f32[97,1,256]{2,1,0:T(1,128)}, f32[97,1,256]{2,1,0:T(1,128)S(1)}, u32[]{:S(2)}, u32[]{:S(2)}) collective-permute-start(f32[97,1,256]{2,1,0:T(1,128)} %get-tuple-element.52), channel_id=1, source_target_pairs={{8,0},{16,8},{24,16},{32,24},{40,32},{48,40},{56,48},{64,56},{72,6... | collective-permute-start | bytes 297992 | tf_op jit(solution)/shard_map/ppermute | solution.py:41
  192.0 5.5 %collective-permute-start.22 = (f32[97,6,1]{2,1,0:T(8,128)S(1)}, f32[97,6,1]{2,1,0:T(8,128)S(1)}, u32[]{:S(2)}, u32[]{:S(2)}) collective-permute-start(f32[97,6,1]{2,1,0:T(8,128)S(1)} %get-tuple-element.47), channel_id=1, source_target_pairs={{0,1},{1,2},{2,3},{3,4},{4,5},{5,6},{6,7},{7,0},{8,9},{9,10},{10,1... | collective-permute-start | bytes 6992 | tf_op jit(solution)/shard_map/ppermute | solution.py:39
  197.5 2.2 collective-permute-start.23
  201.8 4.9 %collective-permute-done.22 = f32[97,6,1]{2,1,0:T(8,128)S(1)} collective-permute-done((f32[97,6,1]{2,1,0:T(8,128)S(1)}, f32[97,6,1]{2,1,0:T(8,128)S(1)}, u32[]{:S(2)}, u32[]{:S(2)}) %collective-permute-start.22) | collective-permute-done | bytes 2360 | tf_op jit(solution)/shard_map/ppermute | solution.py:39
  208.3 5.5 %collective-permute-done.23 = f32[97,6,1]{2,1,0:T(8,128)} collective-permute-done((f32[97,6,1]{2,1,0:T(8,128)}, f32[97,6,1]{2,1,0:T(8,128)}, u32[]{:S(2)}, u32[]{:S(2)}) %collective-permute-start.23) | collective-permute-done | bytes 2360 | tf_op jit(solution)/shard_map/ppermute | solution.py:41
  (286 shorter events, 81.5 us)
Async XLA Ops:
  0.6 11.0 %copy-start.43 = (s32[4,256]{1,0:T(4,128)S(1)}, s32[4,256]{1,0:T(4,128)}, u32[]{:S(2)}) copy-start(s32[4,256]{1,0:T(4,128)} %param.52) | copy-start | bytes 12292
  0.6 27.2 %copy-start = (f32[16,6,4,256]{3,2,1,0:T(4,128)S(1)}, f32[16,6,4,256]{3,2,1,0:T(4,128)}, u32[]{:S(2)}) copy-start(f32[16,6,4,256]{3,2,1,0:T(4,128)} %param.46) | copy-start | bytes 1179652
  1.4 38.7 %collective-permute-start.2 = (f32[2,1,256]{2,1,0:T(1,128)S(1)}, f32[2,1,256]{2,1,0:T(1,128)S(1)}, u32[]{:S(2)}, u32[]{:S(2)}) collective-permute-start(f32[2,1,256]{2,1,0:T(1,128)S(1)} %slice.455), channel_id=1, source_target_pairs={{8,0},{16,8},{24,16},{32,24},{40,32},{48,40},{56,48},{64,56},{72,6... | collective-permute-start | bytes 6152 | tf_op jit(solution)/shard_map/ppermute | solution.py:23
  11.9 18.8 %collective-permute-start = (f32[1,5]{1,0:T(1,128)S(1)}, f32[1,5]{1,0:T(1,128)S(1)}, u32[]{:S(2)}, u32[]{:S(2)}) collective-permute-start(f32[1,5]{1,0:T(1,128)S(1)} %bitcast.344), channel_id=1, source_target_pairs={{0,1},{1,2},{2,3},{3,4},{4,5},{5,6},{6,7},{7,0},{8,9},{9,10},{10,1... | collective-permute-start | bytes 68 | tf_op jit(solution)/shard_map/ppermute | solution.py:29
  17.4 85.1 %collective-permute-start.12 = (f32[97,1,256]{2,1,0:T(1,128)}, f32[97,1,256]{2,1,0:T(1,128)S(1)}, u32[]{:S(2)}, u32[]{:S(2)}) collective-permute-start(f32[97,1,256]{2,1,0:T(1,128)} %get-tuple-element.57), channel_id=1, source_target_pairs={{0,8},{8,16},{16,24},{24,32},{32,40},{40,48},{48,56},{56,64},{64,7... | collective-permute-start | bytes 297992 | tf_op jit(solution)/shard_map/ppermute | solution.py:39
  19.3 83.4 %collective-permute-start.13 = (f32[97,1,256]{2,1,0:T(1,128)}, f32[97,1,256]{2,1,0:T(1,128)}, u32[]{:S(2)}, u32[]{:S(2)}) collective-permute-start(f32[97,1,256]{2,1,0:T(1,128)} %get-tuple-element.56), channel_id=1, source_target_pairs={{8,0},{16,8},{24,16},{32,24},{40,32},{48,40},{56,48},{64,56},{72,6... | collective-permute-start | bytes 297992 | tf_op jit(solution)/shard_map/ppermute | solution.py:41
  30.9 9.1 %collective-permute-start.1 = (f32[1,256]{1,0:T(1,128)S(1)}, f32[1,256]{1,0:T(1,128)S(1)}, u32[]{:S(2)}, u32[]{:S(2)}) collective-permute-start(f32[1,256]{1,0:T(1,128)S(1)} %maximum_bitcast_fusion), channel_id=1, source_target_pairs={{0,8},{8,16},{16,24},{24,32},{32,40},{40,48},{48,56},{56,64},{64,7... | collective-permute-start | bytes 3080 | tf_op jit(solution)/shard_map/ppermute | solution.py:23
  40.1 5.5 %collective-permute-start.3 = (f32[2,5,1]{2,1,0:T(8,128)S(1)}, f32[2,5,1]{2,1,0:T(8,128)S(1)}, u32[]{:S(2)}, u32[]{:S(2)}) collective-permute-start(f32[2,5,1]{2,1,0:T(8,128)S(1)} %fusion.113), channel_id=1, source_target_pairs={{0,7},{1,0},{2,1},{3,2},{4,3},{5,4},{6,5},{7,6},{8,15},{9,8},{10,9... | collective-permute-start | bytes 128 | tf_op jit(solution)/shard_map/ppermute | solution.py:29
  47.3 6.4 %collective-permute-start.4 = (f32[2,5]{1,0:T(2,128)S(1)}, f32[2,5]{1,0:T(2,128)S(1)}, u32[]{:S(2)}, u32[]{:S(2)}) collective-permute-start(f32[2,5]{1,0:T(2,128)S(1)} %slice_reduce_fusion.9), channel_id=1, source_target_pairs={{0,1},{1,2},{2,3},{3,4},{4,5},{5,6},{6,7},{7,0},{8,9},{9,10},{10,1... | collective-permute-start | bytes 128 | tf_op jit(solution)/shard_map/ppermute | solution.py:29
  53.9 9.1 %collective-permute-start.5 = (f32[2,256]{1,0:T(2,128)S(1)}, f32[2,256]{1,0:T(2,128)S(1)}, u32[]{:S(2)}, u32[]{:S(2)}) collective-permute-start(f32[2,256]{1,0:T(2,128)S(1)} %bitcast.340), channel_id=1, source_target_pairs={{0,8},{8,16},{16,24},{24,32},{32,40},{40,48},{48,56},{56,64},{64,7... | collective-permute-start | bytes 6152 | tf_op jit(solution)/shard_map/ppermute | solution.py:23
  63.1 3.2 %collective-permute-start.6 = (f32[2,1,256]{2,1,0:T(1,128)S(1)}, f32[2,1,256]{2,1,0:T(1,128)S(1)}, u32[]{:S(2)}, u32[]{:S(2)}) collective-permute-start(f32[2,1,256]{2,1,0:T(1,128)S(1)} %slice.594), channel_id=1, source_target_pairs={{8,0},{16,8},{24,16},{32,24},{40,32},{48,40},{56,48},{64,56},{72,6... | collective-permute-start | bytes 6152 | tf_op jit(solution)/shard_map/ppermute | solution.py:23
  66.3 5.5 %collective-permute-start.7 = (f32[2,5,1]{2,1,0:T(8,128)S(1)}, f32[2,5,1]{2,1,0:T(8,128)S(1)}, u32[]{:S(2)}, u32[]{:S(2)}) collective-permute-start(f32[2,5,1]{2,1,0:T(8,128)S(1)} %fusion.112), channel_id=1, source_target_pairs={{0,7},{1,0},{2,1},{3,2},{4,3},{5,4},{6,5},{7,6},{8,15},{9,8},{10,9... | collective-permute-start | bytes 128 | tf_op jit(solution)/shard_map/ppermute | solution.py:29
  72.9 6.4 %collective-permute-start.8 = (f32[2,5]{1,0:T(2,128)S(1)}, f32[2,5]{1,0:T(2,128)S(1)}, u32[]{:S(2)}, u32[]{:S(2)}) collective-permute-start(f32[2,5]{1,0:T(2,128)S(1)} %slice_reduce_fusion.8), channel_id=1, source_target_pairs={{0,1},{1,2},{2,3},{3,4},{4,5},{5,6},{6,7},{7,0},{8,9},{9,10},{10,1... | collective-permute-start | bytes 128 | tf_op jit(solution)/shard_map/ppermute | solution.py:29
  79.4 9.1 %collective-permute-start.9 = (f32[2,256]{1,0:T(2,128)S(1)}, f32[2,256]{1,0:T(2,128)S(1)}, u32[]{:S(2)}, u32[]{:S(2)}) collective-permute-start(f32[2,256]{1,0:T(2,128)S(1)} %bitcast.339), channel_id=1, source_target_pairs={{0,8},{8,16},{16,24},{24,32},{32,40},{40,48},{48,56},{56,64},{64,7... | collective-permute-start | bytes 6152 | tf_op jit(solution)/shard_map/ppermute | solution.py:23
  88.7 8.8 %copy-start.8 = (f32[2,4,256]{2,1,0:T(4,128)}, f32[2,4,256]{2,1,0:T(4,128)S(1)}, u32[]{:S(2)}) copy-start(f32[2,4,256]{2,1,0:T(4,128)S(1)} %fusion.120) | copy-start | bytes 24580
  88.7 3.2 %collective-permute-start.10 = (f32[2,1,256]{2,1,0:T(1,128)S(1)}, f32[2,1,256]{2,1,0:T(1,128)S(1)}, u32[]{:S(2)}, u32[]{:S(2)}) collective-permute-start(f32[2,1,256]{2,1,0:T(1,128)S(1)} %slice.607), channel_id=1, source_target_pairs={{8,0},{16,8},{24,16},{32,24},{40,32},{48,40},{56,48},{64,56},{72,6... | collective-permute-start | bytes 6152 | tf_op jit(solution)/shard_map/ppermute | solution.py:23
  91.9 5.5 %collective-permute-start.11 = (f32[2,5,1]{2,1,0:T(8,128)S(1)}, f32[2,5,1]{2,1,0:T(8,128)S(1)}, u32[]{:S(2)}, u32[]{:S(2)}) collective-permute-start(f32[2,5,1]{2,1,0:T(8,128)S(1)} %fusion.111), channel_id=1, source_target_pairs={{0,7},{1,0},{2,1},{3,2},{4,3},{5,4},{6,5},{7,6},{8,15},{9,8},{10,9... | collective-permute-start | bytes 128 | tf_op jit(solution)/shard_map/ppermute | solution.py:29
  101.7 69.5 %copy-start.2 = (f32[3,4,257]{2,0,1:T(4,128)}, f32[3,4,257]{2,0,1:T(4,128)S(1)}, u32[]{:S(2)}) copy-start(f32[3,4,257]{2,0,1:T(4,128)S(1)} %get-tuple-element.77) | copy-start | bytes 37012
  104.9 7.5 %copy-start.24 = (f32[3,6,1]{1,0,2:T(4,128)S(1)}, f32[3,6,1]{1,0,2:T(4,128)}, u32[]{:S(2)}) copy-start(f32[3,6,1]{1,0,2:T(4,128)} %constant.131) | copy-start | bytes 220
  105.1 8.4 %copy-start.1 = (f32[16,3,4,256]{3,1,2,0:T(4,128)S(1)}, f32[16,3,4,256]{3,1,2,0:T(4,128)}, u32[]{:S(2)}) copy-start(f32[16,3,4,256]{3,1,2,0:T(4,128)} %get-tuple-element.45) | copy-start | bytes 589828
  105.1 13.4 %collective-permute-start.14 = (f32[97,6,1]{2,0,1:T(8,128)S(1)}, f32[97,6,1]{2,0,1:T(8,128)S(1)}, u32[]{:S(2)}, u32[]{:S(2)}) collective-permute-start(f32[97,6,1]{2,0,1:T(8,128)S(1)} %get-tuple-element.51), channel_id=1, source_target_pairs={{0,1},{1,2},{2,3},{3,4},{4,5},{5,6},{6,7},{7,0},{8,9},{9,10},{10,1... | collective-permute-start | bytes 6992 | tf_op jit(solution)/shard_map/ppermute | solution.py:39
  109.5 13.8 %collective-permute-start.15 = (f32[97,6,1]{2,0,1:T(8,128)S(1)}, f32[97,6,1]{2,0,1:T(8,128)}, u32[]{:S(2)}, u32[]{:S(2)}) collective-permute-start(f32[97,6,1]{2,0,1:T(8,128)S(1)} %get-tuple-element.50), channel_id=1, source_target_pairs={{1,0},{2,1},{3,2},{4,3},{5,4},{6,5},{7,6},{0,7},{9,8},{10,9},{11,1... | collective-permute-start | bytes 6992 | tf_op jit(solution)/shard_map/ppermute | solution.py:41
  134.1 10.6 %collective-permute-start.16 = (f32[97,1,256]{2,1,0:T(1,128)S(1)}, f32[97,1,256]{2,1,0:T(1,128)S(1)}, u32[]{:S(2)}, u32[]{:S(2)}) collective-permute-start(f32[97,1,256]{2,1,0:T(1,128)S(1)} %get-tuple-element.55), channel_id=1, source_target_pairs={{0,8},{8,16},{16,24},{24,32},{32,40},{40,48},{48,56},{56,64},{64,7... | collective-permute-start | bytes 297992 | tf_op jit(solution)/shard_map/ppermute | solution.py:39
  136.2 10.4 %collective-permute-start.17 = (f32[97,1,256]{2,1,0:T(1,128)}, f32[97,1,256]{2,1,0:T(1,128)S(1)}, u32[]{:S(2)}, u32[]{:S(2)}) collective-permute-start(f32[97,1,256]{2,1,0:T(1,128)} %get-tuple-element.54), channel_id=1, source_target_pairs={{8,0},{16,8},{24,16},{32,24},{40,32},{48,40},{56,48},{64,56},{72,6... | collective-permute-start | bytes 297992 | tf_op jit(solution)/shard_map/ppermute | solution.py:41
  148.1 8.0 %copy-start.38 = (f32[5]{0:T(128)S(1)}, f32[5]{0:T(128)}, u32[]{:S(2)}) copy-start(f32[5]{0:T(128)} %pad_maximum_fusion.31) | copy-start | bytes 64
  148.1 8.1 %copy-start.7 = (f32[16,3,1,256]{3,1,2,0:T(4,128)S(1)}, f32[16,3,1,256]{3,1,2,0:T(4,128)}, u32[]{:S(2)}) copy-start(f32[16,3,1,256]{3,1,2,0:T(4,128)} %convolution_bitcast_fusion.9) | copy-start | bytes 147460
  149.0 12.9 %collective-permute-start.18 = (f32[97,6,1]{2,1,0:T(8,128)S(1)}, f32[97,6,1]{2,1,0:T(8,128)S(1)}, u32[]{:S(2)}, u32[]{:S(2)}) collective-permute-start(f32[97,6,1]{2,1,0:T(8,128)S(1)} %get-tuple-element.49), channel_id=1, source_target_pairs={{0,1},{1,2},{2,3},{3,4},{4,5},{5,6},{6,7},{7,0},{8,9},{9,10},{10,1... | collective-permute-start | bytes 6992 | tf_op jit(solution)/shard_map/ppermute | solution.py:39
  153.1 14.3 %collective-permute-start.19 = (f32[97,6,1]{2,1,0:T(8,128)}, f32[97,6,1]{2,1,0:T(8,128)}, u32[]{:S(2)}, u32[]{:S(2)}) collective-permute-start(f32[97,6,1]{2,1,0:T(8,128)} %get-tuple-element.48), channel_id=1, source_target_pairs={{1,0},{2,1},{3,2},{4,3},{5,4},{6,5},{7,6},{0,7},{9,8},{10,9},{11,1... | collective-permute-start | bytes 6992 | tf_op jit(solution)/shard_map/ppermute | solution.py:41
  177.9 10.2 %collective-permute-start.20 = (f32[97,1,256]{2,1,0:T(1,128)S(1)}, f32[97,1,256]{2,1,0:T(1,128)S(1)}, u32[]{:S(2)}, u32[]{:S(2)}) collective-permute-start(f32[97,1,256]{2,1,0:T(1,128)S(1)} %get-tuple-element.53), channel_id=1, source_target_pairs={{0,8},{8,16},{16,24},{24,32},{32,40},{40,48},{48,56},{56,64},{64,7... | collective-permute-start | bytes 297992 | tf_op jit(solution)/shard_map/ppermute | solution.py:39
  180.0 10.4 %collective-permute-start.21 = (f32[97,1,256]{2,1,0:T(1,128)}, f32[97,1,256]{2,1,0:T(1,128)S(1)}, u32[]{:S(2)}, u32[]{:S(2)}) collective-permute-start(f32[97,1,256]{2,1,0:T(1,128)} %get-tuple-element.52), channel_id=1, source_target_pairs={{8,0},{16,8},{24,16},{32,24},{40,32},{48,40},{56,48},{64,56},{72,6... | collective-permute-start | bytes 297992 | tf_op jit(solution)/shard_map/ppermute | solution.py:41
  192.0 14.6 %collective-permute-start.22 = (f32[97,6,1]{2,1,0:T(8,128)S(1)}, f32[97,6,1]{2,1,0:T(8,128)S(1)}, u32[]{:S(2)}, u32[]{:S(2)}) collective-permute-start(f32[97,6,1]{2,1,0:T(8,128)S(1)} %get-tuple-element.47), channel_id=1, source_target_pairs={{0,1},{1,2},{2,3},{3,4},{4,5},{5,6},{6,7},{7,0},{8,9},{9,10},{10,1... | collective-permute-start | bytes 6992 | tf_op jit(solution)/shard_map/ppermute | solution.py:39
  197.5 16.2 %collective-permute-start.23 = (f32[97,6,1]{2,1,0:T(8,128)}, f32[97,6,1]{2,1,0:T(8,128)}, u32[]{:S(2)}, u32[]{:S(2)}) collective-permute-start(f32[97,6,1]{2,1,0:T(8,128)} %get-tuple-element.46), channel_id=1, source_target_pairs={{1,0},{2,1},{3,2},{4,3},{5,4},{6,5},{7,6},{0,7},{9,8},{10,9},{11,1... | collective-permute-start | bytes 6992 | tf_op jit(solution)/shard_map/ppermute | solution.py:41
  (41 other events, 56.4 us)
where the time goes:
time: 222 us; the launch traced here: 220 us
  starting transfers between devices  92.9 us (42%)
  waiting for transfers between devices  58.6 us (26%)
  local copies, waits for them, and re-layouts  33.7 us (15%)
  matrix products  24.3 us (11%)
  other arithmetic  8.39 us (4%)
    ppermute x6, starting transfers between devices, with_halo(): lax.ppermute(head, axis, [((i + 1) % count, i) for i in range(count)])  31.4 us
    dot_general x37, matrix products, contract(): return jnp.einsum(form, left, right, precision=lax.Precision.HIGHEST)  24.3 us
    ppermute x6, waiting for transfers between devices, shifted(): return lax.ppermute(x, axis, pairs)  22.4 us
    ppermute x6, starting transfers between devices, passed_along(): return lax.ppermute(value, axis, pairs)  22 us
    ppermute x6, starting transfers between devices, shifted(): return lax.ppermute(x, axis, pairs)  19.8 us
    ppermute x6, starting transfers between devices, with_halo(): lax.ppermute(tail, axis, [(i, (i + 1) % count) for i in range(count)])  19.7 us
    unnamed x103, local copies, waits for them, and re-layouts  14.5 us
    ppermute x6, waiting for transfers between devices, with_halo(): lax.ppermute(head, axis, [((i + 1) % count, i) for i in range(count)])  13.6 us
  transfers between devices with their start and end apart: 24, of which 20 were waited for; matrix products, arithmetic and copies ran while one was open for 10% of the time, Pallas kernels for 0%

commit v1 on v0

v1 whole, which is shorter than its diff:
```python
import functools
import math

import jax
import jax.numpy as jnp
from jax import lax
from jax.experimental import pallas as pl
from jax.experimental.pallas import tpu as pltpu
from jax.sharding import PartitionSpec as P

MESH = pl.DeviceIdType.MESH
F32 = jnp.float32
NTR, ROWS, COLS = 16, 4, 256
ITERS = 2
GAUSS = math.sqrt(0.6)
DT = 0.15
THIRD = 1.0 / 3.0
VEL, STRESS, STRENGTH, MASS, WIND, OCEAN, FIELDS = 0, 2, 5, 6, 7, 9, 10
VOL, NORTH, EAST, LAND, COEFS = 0, 24, 27, 30, 31
SLOT = (0, 8, 64, 72)
AROUND = ((0, -1), (0, 1), (-1, 0), (1, 0), (-1, -1), (-1, 1), (1, -1), (1, 1))


def lanes(shape):
    return lax.broadcasted_iota(jnp.int32, shape, len(shape) - 1)


def sublanes(shape):
    return lax.broadcasted_iota(jnp.int32, shape, len(shape) - 2)


def turn(x, by, axis):
    by = by % x.shape[axis] if isinstance(by, int) else by
    return x if isinstance(by, int) and by == 0 else pltpu.roll(x, by, axis)


def line_traces(a, b, mid, along, across, cross):
    base = a + b
    outer = base + 0.4 * mid
    inner = base - 0.5 * mid
    slope_high = along + cross
    slope_low = along - cross
    high = outer + across
    low = outer - across
    return (
        (high - slope_high, inner + across, high + slope_high),
        (low - slope_low, inner - across, low + slope_low),
    )


def row_traces(c):
    return line_traces(c[0], c[5], c[3], GAUSS * c[1], c[2], GAUSS * c[4])


def col_traces(c):
    return line_traces(c[0], c[3], c[5], GAUSS * c[2], c[1], GAUSS * c[4])


def face_moments(weights, inside, outside):
    f = [w * jnp.where(w > 0.0, a, b) for w, a, b in zip(weights, inside, outside)]
    both = f[0] + f[2]
    return (both + f[1], f[2] - f[0], 0.4 * both - 0.5 * f[1])


def rate(c, k, north, south, east, west):
    d_row = [s - n for s, n in zip(south, north)]
    d_col = [w - e for w, e in zip(west, east)]
    sum_row = [south[i] + north[i] for i in range(2)]
    sum_col = [west[i] + east[i] for i in range(2)]
    g0 = d_row[0] + d_col[0]
    g1 = k(0) * c[0] + k(1) * c[1] + k(2) * c[2] + k(3) * c[4] + (3.0 * GAUSS) * d_row[1] - 3.0 * sum_col[0]
    g2 = k(4) * c[0] + k(5) * c[1] + k(6) * c[2] + k(7) * c[4] + (3.0 * GAUSS) * d_col[1] - 3.0 * sum_row[0]
    g3 = k(8) * c[1] + k(9) * c[0] + k(10) * c[3] + k(11) * c[4] + k(12) * c[2] + 5.0 * (d_row[2] + d_col[0])
    g5 = k(13) * c[2] + k(14) * c[0] + k(15) * c[5] + k(16) * c[4] + k(17) * c[1] + 5.0 * (d_row[0] + d_col[2])
    g4 = (
        k(18) * c[0] + k(19) * c[1] + k(20) * c[2] + k(21) * c[3] + k(22) * c[4] + k(23) * c[5]
        - (9.0 * GAUSS) * (sum_row[1] + sum_col[1])
    )
    return (g0, g1, g2, g3, g4, g5)


def kernel(
    nlat, nlon,
    tr, vel, stress, strength, mass, wind, mask,
    o_vel, o_str, o_tr,
    raw, mp, mski, mps, mpn, vn2, ep, lep, q, lq, c0, ts, tn, tup, tdown, c1, c2, kf, ks, st, st1, sx, fl,
    lsem, ssem, rsem,
):
    lat = lax.axis_index("lat")
    lon = lax.axis_index("lon")
    east = lax.rem(lon + 1, nlon)
    west = lax.rem(lon + nlon - 1, nlon)
    has = {1: lat < nlat - 1, -1: lat > 0, -2: lat > 1, 2: lat < nlat - 2}

    def device(dlat, dlon):
        return (lat + dlat, {0: lon, 1: east, -1: west}[dlon])

    def given(dlat, act):
        if dlat == 0:
            act()
        else:
            pl.when(has[dlat])(act)

    local = [
        pltpu.make_async_copy(src, dst, lsem.at[i])
        for i, (src, dst) in enumerate(
            [
                (vel, mp.at[pl.ds(VEL, 2)]),
                (stress, mp.at[pl.ds(STRESS, 3)]),
                (strength, mp.at[STRENGTH]),
                (mass, mp.at[MASS]),
                (wind, mp.at[pl.ds(WIND, 2)]),
                (mask, mski),
                (tr.at[pl.ds(0, 384)], raw.at[pl.ds(0, 384)]),
                (tr.at[pl.ds(384, 384)], raw.at[pl.ds(384, 384)]),
            ]
        )
    ]

    barrier = pltpu.get_barrier_semaphore()

    def greet(dlat):
        for dlon in (0, 1, -1):
            if dlat or dlon:
                pl.semaphore_signal(barrier, inc=1, device_id=device(dlat, dlon), device_id_type=MESH)

    for dlat in (1, 0, -1, 2):
        given(dlat, functools.partial(greet, dlat))
    for copy in local:
        copy.start()

    table = []

    def message(src, dst, dlat, dlon):
        i = len(table)
        table.append((
            dlat,
            pltpu.make_async_remote_copy(
                src_ref=src, dst_ref=dst, send_sem=ssem.at[i], recv_sem=rsem.at[i],
                device_id=device(dlat, dlon), device_id_type=MESH,
            ),
        ))
        return i

    first = []
    for dlat in (1, -1, 0, -2):
        for dlon in (1, -1):
            first.append(message(ep, lep.at[0 if dlon < 0 else 1, {1: 0, 0: 1, -1: 2, -2: 3}[dlat]], dlat, dlon))
    first.append(message(mp, mps, 1, 0))
    first.append(message(mp, mpn, -1, 0))
    first.append(message(mp.at[pl.ds(VEL, 2)], vn2, -2, 0))
    edges = [message(q, lq.at[AROUND.index((-dlat, -dlon))], dlat, dlon) for dlat, dlon in AROUND]
    bulk = []
    for g in range(2):
        bulk.append([
            message(c0.at[g, pl.ds(4, 2)], c0.at[g, pl.ds(0, 2)], 1, 0),
            message(c0.at[g, pl.ds(2, 2)], c0.at[g, pl.ds(6, 2)], -1, 0),
            message(tup.at[g], ts.at[g], 1, 0),
            message(tdown.at[g], tn.at[g], -1, 0),
        ])

    def send(some):
        for dlat in (1, -1, 0, -2):
            mine = [i for i in some if table[i][0] == dlat]
            if mine:
                given(dlat, lambda mine=mine: [table[i][1].start() for i in mine] and None)

    def arrive(some):
        for dlat in (0, 1, -1, -2):
            mine = [i for i in some if table[i][0] == dlat]
            if mine:
                given(-dlat, lambda mine=mine: [table[i][1].wait_recv() for i in mine] and None)

    def sent(some):
        for dlat in (0, 1, -1, -2):
            mine = [i for i in some if table[i][0] == dlat]
            if mine:
                given(dlat, lambda mine=mine: [table[i][1].wait_send() for i in mine] and None)

    def clear(row, trace, steps):
        for g in range(2):
            for i in (row, row + 1):
                for k in range(6):
                    c0[g, i, k] = jnp.zeros((8, COLS), F32)
            for i in range(3):
                trace[g, i] = jnp.zeros((8, COLS), F32)
        for n, (dlat, _) in enumerate(AROUND):
            if dlat == steps:
                for m in range(3):
                    lq[n, m] = jnp.zeros((8, 128), F32)

    pl.when(lat == 0)(lambda: clear(0, ts, -1))
    pl.when(lat == nlat - 1)(lambda: clear(6, tn, 1))

    for copy in local[:6]:
        copy.wait()
    mp[OCEAN] = mski[...].astype(F32)
    at4 = lanes((4, 128))
    for h in range(2):
        acc = jnp.zeros((4, 128), F32)
        for f in range(8 * h, min(8 * h + 8, FIELDS)):
            p = 16 * (f % 8)
            x = mp[f]
            acc = jnp.where((at4 >= p) & (at4 < p + 8), turn(x[:, :128], p, 1), acc)
            acc = jnp.where((at4 >= p + 8) & (at4 < p + 16), turn(x[:, 128:], p + 16, 1), acc)
        ep[h] = acc

    one = jnp.int32(1)
    zero = jnp.int32(0)
    targets = 2 + 3 * (jnp.where(has[1], one, zero) + jnp.where(has[-1], one, zero) + jnp.where(has[-2], one, zero))
    pl.semaphore_wait(barrier, targets)
    send(first)

    def lay_out(g):
        def row(i, _):
            for k in range(6):
                for t in range(2):
                    c0[g, i + 2, k, :, t * 128:(t + 1) * 128] = raw[pl.ds(g * 384 + k * 8 + t * 4 + i, 8, stride=48), :]
            return 0

        lax.fori_loop(0, ROWS, row, 0)
        for i in range(3):
            pass
        up = row_traces([c0[g, 3, k] for k in range(6)])[0]
        down = row_traces([c0[g, 4, k] for k in range(6)])[1]
        for i in range(3):
            tup[g, i] = up[i]
            tdown[g, i] = down[i]

    at8 = lanes((8, 128))
    in_row = at8 % 16

    def pack_edges(m, _):
        acc = None
        for j in range(4):
            s = 4 * m + j
            g, k = s // 6, s % 6
            strip = jnp.zeros((8, 128), F32)
            for i in range(ROWS):
                x = c0[g, i + 2, k]
                x = jnp.where(at8 < 4, x[:, :128], turn(x[:, 128:], 8, 1))
                p = 16 * (i + 2) + 4
                strip = jnp.where((at8 >= p) & (at8 < p + 8), turn(x, p, 1), strip)
            st[s] = strip
            acc = strip if acc is None else acc + turn(strip, SLOT[j], 1)
        q[m] = acc
        return 0

    local[6].wait()
    lay_out(0)
    send(bulk[0])
    local[7].wait()
    lay_out(1)
    lax.fori_loop(0, 3, pack_edges, 0)
    send(edges)
    send(bulk[1])

    arrive(first)
    wide = (16, 384)
    grow = 4 * lat - 4 + sublanes(wide)
    inside = (grow >= 0) & (grow < 4 * nlat)
    packed = [[jnp.concatenate([lep[s, r, h] for r in range(4)], 0) for h in range(2)] for s in range(2)]
    at16 = lanes((16, 128))

    def extended(f):
        h, p = f // 8, 16 * (f % 8)
        north2 = vn2[f - VEL] if f < VEL + 2 else jnp.zeros((4, COLS), F32)
        here = jnp.concatenate([mps[f], mp[f], mpn[f], north2], 0)
        side = jnp.where(at16 < 64, turn(packed[0][h], -p, 1), turn(packed[1][h], 112 - p, 1))
        return jnp.where(inside, jnp.concatenate([here, side], 1), 0.0)

    def above(x):
        return turn(x, -1, 0)

    def below(x):
        return turn(x, 1, 0)

    def right(x):
        return turn(x, -1, 1)

    def left(x):
        return turn(x, 1, 1)

    f = [extended(i) for i in range(FIELDS)]
    start = f[VEL:VEL + 2]
    moving = f[VEL:VEL + 2]
    current = f[STRESS:STRESS + 3]
    power, weight, push, ocean = f[STRENGTH], f[MASS], f[WIND:WIND + 2], f[OCEAN]
    count = ocean + below(ocean)
    count = count + left(count)
    active = jnp.where((grow > 0) & (grow < 4 * nlat), jnp.minimum(count, 1.0), 0.0)
    scale = active / (4.0 + weight)
    fixed = [start[i] + weight * push[i] for i in range(2)]

    def slopes(x):
        total, diff = x + above(x), above(x) - x
        return 0.5 * (right(total) - total), 0.5 * (diff + right(diff))

    def force(along, across):
        p = along + below(along)
        r = across - below(across)
        return 0.5 * ((p - left(p)) + (r + left(r)))

    for _ in range(ITERS):
        e11, ux_y = slopes(moving[0])
        uy_x, e22 = slopes(moving[1])
        e12 = 0.5 * (ux_y + uy_x)
        inner = (e11 * e11 + e22 * e22) * 1.25 + e12 * e12 + 1.5 * e11 * e22 + 0.01
        zeta = 0.5 * power / jnp.sqrt(inner)
        shear = 0.25 * zeta
        spread = (zeta - shear) * (e11 + e22) - 0.5 * power
        plastic = (2.0 * shear * e11 + spread, 2.0 * shear * e22 + spread, 2.0 * shear * e12)
        current = [ocean * (a + (b - a) * THIRD) for a, b in zip(current, plastic)]
        s11, s22, s12 = current
        pushed = (force(s11, s12), force(s12, s22))
        moving = [scale * (3.0 * moving[i] + fixed[i] + weight * pushed[i]) for i in range(2)]

    for i in range(2):
        o_vel[i] = moving[i][4:8, :COLS]
    for i in range(3):
        o_str[i] = current[i][4:8, :COLS]

    def modes(x):
        total, diff = x + above(x), above(x) - x
        rt, rd = right(total), right(diff)
        w = (0.25 * DT) * ocean
        return w * (total + rt), w * (rt - total), w * (diff + rd), w * (rd - diff)

    def normals(a, b, act):
        mean, half = 0.5 * (a + b), (0.5 * GAUSS) * (b - a)
        return ((5.0 / 9.0) * act * (mean - half), (8.0 / 9.0) * act * mean, (5.0 / 9.0) * act * (mean + half))

    u0, u1, u2, u3 = modes(moving[0])
    v0, v1, v2, v3 = modes(moving[1])
    vn = above(moving[1])
    ue = right(moving[0])
    coefs = [
        3.0 * u0, u1, u2, THIRD * u3,
        3.0 * v0, v1, v2, THIRD * v3,
        5.0 * u0, 5.0 * u1, 2.0 * u1, (5.0 * THIRD) * u2, (5.0 * THIRD) * u3,
        5.0 * v0, 5.0 * v2, 2.0 * v2, (5.0 * THIRD) * v1, (5.0 * THIRD) * v3,
        3.0 * (u2 + v1), 3.0 * v0 + u3, 3.0 * u0 + v3, 1.2 * v1, u1 + v2, 1.2 * u2,
    ]
    coefs += normals(vn, right(vn), (0.25 * DT) * ocean * above(ocean))
    coefs += normals(ue, above(ue), (0.25 * DT) * ocean * right(ocean))
    coefs.append(ocean)
    own_lanes = (at8 // 16) == sublanes((8, 128))
    for i, x in enumerate(coefs):
        kf[i] = x[:, :COLS]
        if i < LAND:
            a, b, c = x[:, :128], x[:, 128:256], x[:, 256:]
            low = turn(jnp.where(at16 >= 124, c, a), 4, 1)
            high = turn(jnp.where(at16 >= 124, b, c), 12, 1)
            z = turn(jnp.where(at16 < 8, low, high), -2, 0)[:8]
            z = jnp.where(own_lanes, pltpu.roll(z, 0, 1, stride=16, stride_axis=0), 0.0)
            for by in (4, 2, 1):
                z = z + turn(z, by, 0)
            ks[i] = z

    arrive(edges)

    def unpack_edges(m, _):
        for j in range(4):
            s = 4 * m + j
            strip = st[s]
            for n, (dlat, dlon) in enumerate(AROUND):
                by = -SLOT[j] + 8 * dlon + 64 * dlat
                ok = {-1: in_row < 4, 0: (in_row >= 4) & (in_row < 12), 1: in_row >= 12}[dlon]
                ok = ok & {-1: at8 < 32, 0: (at8 >= 32) & (at8 < 96), 1: at8 >= 96}[dlat]
                strip = jnp.where(ok, turn(lq[n, m], by, 1), strip)
            st[s] = strip
        return 0

    lax.fori_loop(0, 3, unpack_edges, 0)

    def strip_columns(c):
        e, w = col_traces(c)
        return face_moments([ks[EAST + i] for i in range(3)], e, [turn(x, -1, 1) for x in w])

    def strip_rate(c):
        n, s = row_traces(c)
        north = face_moments([ks[NORTH + i] for i in range(3)], n, [turn(x, -16, 1) for x in s])
        east_m = strip_columns(c)
        g = rate(c, lambda i: ks[VOL + i], north, [turn(x, 16, 1) for x in north], east_m, [turn(x, 1, 1) for x in east_m])
        return g, east_m

    lane = lanes((8, COLS))

    for g in range(2):
        base = [st[6 * g + k] for k in range(6)]
        r, m = strip_rate(base)
        for i in range(3):
            sx[0, i] = m[i]
        now = [a + b for a, b in zip(base, r)]
        r, m = strip_rate(now)
        for i in range(3):
            sx[1, i] = m[i]
        now = [0.75 * a + 0.25 * (b + d) for a, b, d in zip(base, now, r)]
        m = strip_columns(now)
        for i in range(3):
            sx[2, i] = m[i]

        arrive(bulk[g])

        for step, (src, low, high) in enumerate(((c0.at[g], 0, 7), (c1, 0, 7), (c2, 1, 6))):

            def faces(i, carry, src=src):
                n, s = row_traces([src[i, k] for k in range(6)])
                w = [kf[NORTH + j, pl.ds(i + 1, 1), :] for j in range(3)]
                w = [jnp.broadcast_to(x, (8, COLS)) for x in w]
                m = face_moments(w, carry, s)
                for j in range(3):
                    fl[i, j] = m[j]
                return n

            if step == 0:
                last = lax.fori_loop(0, 8, faces, tuple(ts[g, j] for j in range(3)))
                w = [jnp.broadcast_to(kf[NORTH + j, 9:10, :], (8, COLS)) for j in range(3)]
                m = face_moments(w, last, [tn[g, j] for j in range(3)])
                for j in range(3):
                    fl[8, j] = m[j]
                rows = (0, 8)
            else:
                n, _ = row_traces([src[low, k] for k in range(6)])
                lax.fori_loop(low + 1, high + 1, faces, n)
                rows = (low + 1, high)

            def update(i, _, src=src, step=step):
                c = [src[i, k] for k in range(6)]

                def k_of(j):
                    return jnp.broadcast_to(kf[j, pl.ds(i + 2, 1), :], (8, COLS))

                e, w = col_traces(c)
                m = face_moments([k_of(EAST + j) for j in range(3)], e, [turn(x, -1, 1) for x in w])
                p = 16 * i
                em, wm = [], []
                for j in range(3):
                    rim = sx[step, j]
                    at_east = pltpu.roll(rim, lax.rem(127 - 11 - p + 256, 128), 1)
                    at_west = pltpu.roll(rim, lax.rem(256 - 3 - p, 128), 1)
                    x = jnp.where(lane == COLS - 1, jnp.concatenate([at_east, at_east], 1), m[j])
                    em.append(x)
                    wm.append(jnp.where(lane == 0, jnp.concatenate([at_west, at_west], 1), turn(x, 1, 1)))
                r = rate(c, k_of, [fl[i + 1, j] for j in range(3)], [fl[i, j] for j in range(3)], em, wm)
                if step == 0:
                    for k in range(6):
                        c1[i, k] = c[k] + r[k]
                elif step == 1:
                    for k in range(6):
                        c2[i, k] = 0.75 * c0[g, i, k] + 0.25 * (c[k] + r[k])
                else:
                    sea = k_of(LAND)
                    for k in range(6):
                        x = sea * (THIRD * c0[g, i, k] + (2.0 * THIRD) * (c[k] + r[k]))
                        for t in range(2):
                            o_tr[pl.ds(g * 384 + k * 8 + t * 4 + i - 2, 8, stride=48), :] = x[:, t * 128:(t + 1) * 128]
                return 0

            lax.fori_loop(*rows, update, 0)

    sent(first)
    sent(edges)
    for some in bulk:
        sent(some)


def local_step(nlat, nlon, tracers, velocity, stress, strength, inverse_mass, wind, ocean_mask):
    linear = tracers.reshape(NTR, 6, ROWS, 2, 128).transpose(0, 1, 3, 2, 4).reshape(768, 128)
    hbm = pl.BlockSpec(memory_space=pltpu.HBM)
    vmem = pl.BlockSpec(memory_space=pltpu.VMEM)
    messages = 8 + 3 + 8 + 8
    new_velocity, new_stress, new_tracers = pl.pallas_call(
        functools.partial(kernel, nlat, nlon),
        out_shape=(
            jax.ShapeDtypeStruct((2, ROWS, COLS), F32),
            jax.ShapeDtypeStruct((3, ROWS, COLS), F32),
            jax.ShapeDtypeStruct((768, 128), F32),
        ),
        in_specs=[hbm] * 7,
        out_specs=(vmem, vmem, vmem),
        scratch_shapes=[
            pltpu.VMEM((768, 128), F32),
            pltpu.VMEM((FIELDS, ROWS, COLS), F32),
            pltpu.VMEM((ROWS, COLS), jnp.int32),
            pltpu.VMEM((FIELDS, ROWS, COLS), F32),
            pltpu.VMEM((FIELDS, ROWS, COLS), F32),
            pltpu.VMEM((2, ROWS, COLS), F32),
            pltpu.VMEM((2, 4, 128), F32),
            pltpu.VMEM((2, 4, 2, 4, 128), F32),
            pltpu.VMEM((3, 8, 128), F32),
            pltpu.VMEM((8, 3, 8, 128), F32),
            pltpu.VMEM((2, 8, 6, 8, COLS), F32),
            pltpu.VMEM((2, 3, 8, COLS), F32),
            pltpu.VMEM((2, 3, 8, COLS), F32),
            pltpu.VMEM((2, 3, 8, COLS), F32),
            pltpu.VMEM((2, 3, 8, COLS), F32),
            pltpu.VMEM((8, 6, 8, COLS), F32),
            pltpu.VMEM((8, 6, 8, COLS), F32),
            pltpu.VMEM((COEFS, 16, COLS), F32),
            pltpu.VMEM((LAND, 8, 128), F32),
            pltpu.VMEM((12, 8, 128), F32),
            pltpu.VMEM((6, 8, 128), F32),
            pltpu.VMEM((3, 3, 8, 128), F32),
            pltpu.VMEM((9, 3, 8, COLS), F32),
            pltpu.SemaphoreType.DMA((8,)),
            pltpu.SemaphoreType.DMA((messages,)),
            pltpu.SemaphoreType.DMA((messages,)),
        ],
        compiler_params=pltpu.CompilerParams(
            collective_id=0, has_side_effects=True, vmem_limit_bytes=48 << 20
        ),
    )(linear, velocity, stress, strength, inverse_mass, wind, ocean_mask)
    new_tracers = new_tracers.reshape(NTR, 6, 2, ROWS, 128).transpose(0, 1, 3, 2, 4).reshape(NTR, 6, ROWS, COLS)
    return new_velocity, new_stress, new_tracers


def solution(mesh):
    in_specs = (
        P(None, None, "lat", "lon"),
        P(None, "lat", "lon"),
        P(None, "lat", "lon"),
        P("lat", "lon"),
        P("lat", "lon"),
        P(None, "lat", "lon"),
        P("lat", "lon"),
    )
    out_specs = (P(None, "lat", "lon"), P(None, "lat", "lon"), P(None, None, "lat", "lon"))
    step = functools.partial(local_step, mesh.shape["lat"], mesh.shape["lon"])
    return jax.shard_map(step, mesh=mesh, in_specs=in_specs, out_specs=out_specs, check_vma=False)
```

time: 222 us -> 39.6 us (0.18)
  the two profiles are of different devices: /device:TPU:34 before, /device:TPU:40 now
where the time goes in v1:
time: 39.6 us; the launch traced here: 39.2 us
  Pallas kernels  31.5 us (80%)
  local copies, waits for them, and re-layouts  7.09 us (18%)
  between operations  0.66 us (2%)
    pallas_call x1, Pallas kernels, local_step(): pl.pallas_call(functools.partial(kernel, nlat, nlon), out_shape=(jax.Shap...  31.5 us
    unnamed x17, local copies, waits for them, and re-layouts  7.09 us

profile of v1, /device:TPU:40, one launch (start us, length us, event | category | flops | bytes accessed | tf_op | source)
XLA Modules:
  0.0 39.2 jit_solution(7454509192162224487)
XLA Ops:
  0.6 0.0 copy-start
  0.6 1.0 %copy-done = f32[16,6,4,256]{3,2,1,0:T(4,128)S(1)} copy-done((f32[16,6,4,256]{3,2,1,0:T(4,128)S(1)}, f32[16,6,4,256]{3,2,1,0:T(4,128)}, u32[]{:S(2)}) %copy-start) | copy-done | bytes 393240
  1.6 0.0 copy-start.1
  1.6 0.7 %copy-done.1 = f32[3,4,256]{2,1,0:T(4,128)S(1)} copy-done((f32[3,4,256]{2,1,0:T(4,128)S(1)}, f32[3,4,256]{2,1,0:T(4,128)}, u32[]{:S(2)}) %copy-start.1) | copy-done | bytes 12312
  2.3 0.0 copy-start.2
  2.3 0.7 %copy-done.2 = f32[2,4,256]{2,1,0:T(4,128)S(1)} copy-done((f32[2,4,256]{2,1,0:T(4,128)S(1)}, f32[2,4,256]{2,1,0:T(4,128)}, u32[]{:S(2)}) %copy-start.2) | copy-done | bytes 8216
  3.0 0.0 copy-start.3
  3.0 0.7 %copy-done.3 = f32[2,4,256]{2,1,0:T(4,128)S(1)} copy-done((f32[2,4,256]{2,1,0:T(4,128)S(1)}, f32[2,4,256]{2,1,0:T(4,128)}, u32[]{:S(2)}) %copy-start.3) | copy-done | bytes 8216
  3.7 0.0 copy-start.4
  3.7 0.7 %copy-done.4 = f32[4,256]{1,0:T(4,128)S(1)} copy-done((f32[4,256]{1,0:T(4,128)S(1)}, f32[4,256]{1,0:T(4,128)}, u32[]{:S(2)}) %copy-start.4) | copy-done | bytes 4120
  4.4 0.0 copy-start.5
  4.4 0.7 %copy-done.5 = f32[4,256]{1,0:T(4,128)S(1)} copy-done((f32[4,256]{1,0:T(4,128)S(1)}, f32[4,256]{1,0:T(4,128)}, u32[]{:S(2)}) %copy-start.5) | copy-done | bytes 4120
  5.1 0.0 copy-start.6
  5.1 0.7 %copy-done.6 = s32[4,256]{1,0:T(4,128)S(1)} copy-done((s32[4,256]{1,0:T(4,128)S(1)}, s32[4,256]{1,0:T(4,128)}, u32[]{:S(2)}) %copy-start.6) | copy-done | bytes 4120
  5.8 31.5 %shard_map.94 = (f32[2,4,256]{2,1,0:T(4,128)S(1)}, f32[3,4,256]{2,1,0:T(4,128)S(1)}, f32[768,128]{1,0:T(8,128)S(1)}) custom-call(f32[768,128]{1,0:T(8,128)S(1)} %bitcast.11, f32[2,4,256]{2,1,0:T(4,128)S(1)} %copy-done.2, f32[3,4,256]{2,1,0:T(4,128)S(1)} %copy-done.1, f32[4,256]{1,0:T(4,128)S(1)} %copy-done.4, f32[4,256]{1,0:T(4,128)S(1)} %copy-done.5, ...), custom_call_target="tpu_custom_call" | custom-call | tf_op jit(solution)/shard_map/pallas_call | solution.py:473
  37.3 0.6 %copy.15 = f32[2,4,256]{2,1,0:T(4,128)} copy(f32[2,4,256]{2,1,0:T(4,128)S(1)} %get-tuple-element.12) | data formatting | bytes 16384
  37.9 0.6 %copy.16 = f32[3,4,256]{2,1,0:T(4,128)} copy(f32[3,4,256]{2,1,0:T(4,128)S(1)} %get-tuple-element.13) | data formatting | bytes 24576
  38.5 0.7 %copy.17 = f32[16,6,4,256]{3,2,1,0:T(4,128)} copy(f32[16,6,4,256]{3,2,1,0:T(4,128)S(1)} %bitcast.10) | data formatting | bytes 786432
Async XLA Ops:
  0.6 1.0 %copy-start = (f32[16,6,4,256]{3,2,1,0:T(4,128)S(1)}, f32[16,6,4,256]{3,2,1,0:T(4,128)}, u32[]{:S(2)}) copy-start(f32[16,6,4,256]{3,2,1,0:T(4,128)} %param.7) | copy-start | bytes 1179652
  1.6 0.7 %copy-start.1 = (f32[3,4,256]{2,1,0:T(4,128)S(1)}, f32[3,4,256]{2,1,0:T(4,128)}, u32[]{:S(2)}) copy-start(f32[3,4,256]{2,1,0:T(4,128)} %stress.1) | copy-start | bytes 36868
  2.3 0.7 %copy-start.2 = (f32[2,4,256]{2,1,0:T(4,128)S(1)}, f32[2,4,256]{2,1,0:T(4,128)}, u32[]{:S(2)}) copy-start(f32[2,4,256]{2,1,0:T(4,128)} %vel.1) | copy-start | bytes 24580
  3.0 0.7 %copy-start.3 = (f32[2,4,256]{2,1,0:T(4,128)S(1)}, f32[2,4,256]{2,1,0:T(4,128)}, u32[]{:S(2)}) copy-start(f32[2,4,256]{2,1,0:T(4,128)} %wind.1) | copy-start | bytes 24580
  3.7 0.7 %copy-start.4 = (f32[4,256]{1,0:T(4,128)S(1)}, f32[4,256]{1,0:T(4,128)}, u32[]{:S(2)}) copy-start(f32[4,256]{1,0:T(4,128)} %strength.1) | copy-start | bytes 12292
  4.4 0.7 %copy-start.5 = (f32[4,256]{1,0:T(4,128)S(1)}, f32[4,256]{1,0:T(4,128)}, u32[]{:S(2)}) copy-start(f32[4,256]{1,0:T(4,128)} %mass.1) | copy-start | bytes 12292
  5.1 0.7 %copy-start.6 = (s32[4,256]{1,0:T(4,128)S(1)}, s32[4,256]{1,0:T(4,128)}, u32[]{:S(2)}) copy-start(s32[4,256]{1,0:T(4,128)} %mask.1) | copy-start | bytes 12292

commit v2 on v1

--- a/solution.py
+++ b/solution.py
@@ -83,7 +83,7 @@
     nlat, nlon,
     tr, vel, stress, strength, mass, wind, mask,
     o_vel, o_str, o_tr,
-    raw, mp, mski, mps, mpn, vn2, ep, lep, q, lq, c0, ts, tn, tup, tdown, c1, c2, kf, ks, st, st1, sx, fl,
+    raw, mp, mski, mps, mpn, vn2, ep, lep, q, lq, c0, ts, tn, tup, tdown, c1, c2, kf, ks, st, sx, fl, lo,
     lsem, ssem, rsem,
 ):
     lat = lax.axis_index("lat")
@@ -150,14 +150,12 @@
     first.append(message(mp, mpn, -1, 0))
     first.append(message(mp.at[pl.ds(VEL, 2)], vn2, -2, 0))
     edges = [message(q, lq.at[AROUND.index((-dlat, -dlon))], dlat, dlon) for dlat, dlon in AROUND]
-    bulk = []
-    for g in range(2):
-        bulk.append([
-            message(c0.at[g, pl.ds(4, 2)], c0.at[g, pl.ds(0, 2)], 1, 0),
-            message(c0.at[g, pl.ds(2, 2)], c0.at[g, pl.ds(6, 2)], -1, 0),
-            message(tup.at[g], ts.at[g], 1, 0),
-            message(tdown.at[g], tn.at[g], -1, 0),
-        ])
+    north_rows = [
+        message(c0.at[5], c0.at[1], 1, 0), message(c0.at[4], c0.at[0], 1, 0), message(tup, ts.at[1], 1, 0),
+    ]
+    south_rows = [
+        message(c0.at[2], c0.at[6], -1, 0), message(c0.at[3], c0.at[7], -1, 0), message(tdown, tn, -1, 0),
+    ]
 
     def send(some):
         for dlat in (1, -1, 0, -2):
@@ -181,7 +179,7 @@
         for g in range(2):
             for i in (row, row + 1):
                 for k in range(6):
-                    c0[g, i, k] = jnp.zeros((8, COLS), F32)
+                    c0[i, g, k] = jnp.zeros((8, COLS), F32)
             for i in range(3):
                 trace[g, i] = jnp.zeros((8, COLS), F32)
         for n, (dlat, _) in enumerate(AROUND):
@@ -189,7 +187,7 @@
                 for m in range(3):
                     lq[n, m] = jnp.zeros((8, 128), F32)
 
-    pl.when(lat == 0)(lambda: clear(0, ts, -1))
+    pl.when(lat == 0)(lambda: clear(0, ts.at[1], -1))
     pl.when(lat == nlat - 1)(lambda: clear(6, tn, 1))
 
     for copy in local[:6]:
@@ -215,45 +213,42 @@
         def row(i, _):
             for k in range(6):
                 for t in range(2):
-                    c0[g, i + 2, k, :, t * 128:(t + 1) * 128] = raw[pl.ds(g * 384 + k * 8 + t * 4 + i, 8, stride=48), :]
+                    c0[i + 2, g, k, :, t * 128:(t + 1) * 128] = raw[pl.ds(g * 384 + k * 8 + t * 4 + i, 8, stride=48), :]
             return 0
 
         lax.fori_loop(0, ROWS, row, 0)
-        for i in range(3):
-            pass
-        up = row_traces([c0[g, 3, k] for k in range(6)])[0]
-        down = row_traces([c0[g, 4, k] for k in range(6)])[1]
+
+    at8 = lanes((8, 128))
+    in_row = at8 % 16
+
+    local[6].wait()
+    lay_out(0)
+    local[7].wait()
+    lay_out(1)
+    send([north_rows[0], south_rows[0]])
+    send([north_rows[1], south_rows[1]])
+    for g in range(2):
+        up = row_traces([c0[3, g, k] for k in range(6)])[0]
+        down = row_traces([c0[4, g, k] for k in range(6)])[1]
         for i in range(3):
             tup[g, i] = up[i]
             tdown[g, i] = down[i]
-
-    at8 = lanes((8, 128))
-    in_row = at8 % 16
-
-    def pack_edges(m, _):
+    for m in range(3):
         acc = None
         for j in range(4):
             s = 4 * m + j
             g, k = s // 6, s % 6
             strip = jnp.zeros((8, 128), F32)
             for i in range(ROWS):
-                x = c0[g, i + 2, k]
+                x = c0[i + 2, g, k]
                 x = jnp.where(at8 < 4, x[:, :128], turn(x[:, 128:], 8, 1))
                 p = 16 * (i + 2) + 4
                 strip = jnp.where((at8 >= p) & (at8 < p + 8), turn(x, p, 1), strip)
             st[s] = strip
             acc = strip if acc is None else acc + turn(strip, SLOT[j], 1)
         q[m] = acc
-        return 0
-
-    local[6].wait()
-    lay_out(0)
-    send(bulk[0])
-    local[7].wait()
-    lay_out(1)
-    lax.fori_loop(0, 3, pack_edges, 0)
     send(edges)
-    send(bulk[1])
+    send([north_rows[2], south_rows[2]])
 
     arrive(first)
     wide = (16, 384)
@@ -359,19 +354,17 @@
 
     arrive(edges)
 
-    def unpack_edges(m, _):
-        for j in range(4):
-            s = 4 * m + j
-            strip = st[s]
-            for n, (dlat, dlon) in enumerate(AROUND):
-                by = -SLOT[j] + 8 * dlon + 64 * dlat
-                ok = {-1: in_row < 4, 0: (in_row >= 4) & (in_row < 12), 1: in_row >= 12}[dlon]
-                ok = ok & {-1: at8 < 32, 0: (at8 >= 32) & (at8 < 96), 1: at8 >= 96}[dlat]
-                strip = jnp.where(ok, turn(lq[n, m], by, 1), strip)
-            st[s] = strip
-        return 0
-
-    lax.fori_loop(0, 3, unpack_edges, 0)
+    reach = []
+    for dlat, dlon in AROUND:
+        ok = {-1: in_row < 4, 0: (in_row >= 4) & (in_row < 12), 1: in_row >= 12}[dlon]
+        reach.append(ok & {-1: at8 < 32, 0: (at8 >= 32) & (at8 < 96), 1: at8 >= 96}[dlat])
+    base = []
+    for s in range(12):
+        strip = st[s]
+        for n, (dlat, dlon) in enumerate(AROUND):
+            strip = jnp.where(reach[n], turn(lq[n, s // 4], -SLOT[s % 4] + 8 * dlon + 64 * dlat, 1), strip)
+        base.append(strip)
+    base = (base[:6], base[6:])
 
     def strip_columns(c):
         e, w = col_traces(c)
@@ -384,99 +377,151 @@
         g = rate(c, lambda i: ks[VOL + i], north, [turn(x, 16, 1) for x in north], east_m, [turn(x, 1, 1) for x in east_m])
         return g, east_m
 
+    now = base
+    rim = []
+    for step in range(2):
+        got = [strip_rate(c) for c in now]
+        rim.append([m for _, m in got])
+        if step == 0:
+            now = [[a + b for a, b in zip(c, r)] for c, (r, _) in zip(now, got)]
+        else:
+            now = [
+                [0.75 * a + 0.25 * (b + d) for a, b, d in zip(c, f, r)] for c, f, (r, _) in zip(base, now, got)
+            ]
+    rim.append([strip_columns(c) for c in now])
+    for step in range(3):
+        for g in range(2):
+            for i in range(3):
+                sx[step, g, i] = rim[step][g][i]
+
     lane = lanes((8, COLS))
-
-    for g in range(2):
-        base = [st[6 * g + k] for k in range(6)]
-        r, m = strip_rate(base)
-        for i in range(3):
-            sx[0, i] = m[i]
-        now = [a + b for a, b in zip(base, r)]
-        r, m = strip_rate(now)
-        for i in range(3):
-            sx[1, i] = m[i]
-        now = [0.75 * a + 0.25 * (b + d) for a, b, d in zip(base, now, r)]
-        m = strip_columns(now)
-        for i in range(3):
-            sx[2, i] = m[i]
-
-        arrive(bulk[g])
-
-        for step, (src, low, high) in enumerate(((c0.at[g], 0, 7), (c1, 0, 7), (c2, 1, 6))):
-
-            def faces(i, carry, src=src):
-                n, s = row_traces([src[i, k] for k in range(6)])
-                w = [kf[NORTH + j, pl.ds(i + 1, 1), :] for j in range(3)]
-                w = [jnp.broadcast_to(x, (8, COLS)) for x in w]
-                m = face_moments(w, carry, s)
+    both = range(2)
+
+    def six(ref, i, g):
+        return [ref[i, g, k] for k in range(6)]
+
+    def spread_row(i):
+        return lambda j: jnp.broadcast_to(kf[j, pl.ds(i + 2, 1), :], (8, COLS))
+
+    def open_face(step, i, g, inside, outside, trace):
+        k = spread_row(i)
+        m = face_moments([k(NORTH + j) for j in range(3)], inside, outside)
+        for j in range(3):
+            fl[step, g, j] = m[j]
+            lo[step, g, j] = trace[j]
+
+    def columns(step, i, g, k, c):
+        e, w = col_traces(c)
+        m = face_moments([k(EAST + j) for j in range(3)], e, [turn(x, -1, 1) for x in w])
+        p = 16 * i
+        em, wm = [], []
+        for j in range(3):
+            r = sx[step, g, j]
+            at_east = pltpu.roll(r, lax.rem(127 - 11 - p + 256, 128), 1)
+            at_west = pltpu.roll(r, lax.rem(256 - 3 - p, 128), 1)
+            x = jnp.where(lane == COLS - 1, jnp.concatenate([at_east, at_east], 1), m[j])
+            em.append(x)
+            wm.append(jnp.where(lane == 0, jnp.concatenate([at_west, at_west], 1), turn(x, 1, 1)))
+        return em, wm
+
+    def wave(w, steps):
+        cur, under, old, cols, tops, lows = {}, {}, {}, {}, {}, {}
+        last = 1 - jnp.minimum(w, 1)
+        k = [spread_row(w + s) for s in range(steps)]
+        below_k = [spread_row(w + s - 1) for s in range(steps)]
+        for s in range(steps):
+            for g in both:
+                cur[s, g] = six((c0, c1, c2)[s], w + s, g)
+                old[s, g] = cur[s, g] if s == 0 else six(c0, w + s, g)
+                tops[s, g] = [fl[s, g, j] for j in range(3)]
+                lows[s, g] = [lo[s, g, j] for j in range(3)]
+        for g in both:
+            n, sth = row_traces(six(c0, jnp.maximum(w - 1, 0), g))
+            under[0, g] = ([jnp.where(w == 0, ts[last, g, j], n[j]) for j in range(3)], sth)
+        for s in range(steps):
+            for g in both:
+                cols[s, g] = columns(s, w + s, g, k[s], cur[s, g])
+        done = {}
+        for s in range(steps):
+            for g in both:
+                n, sth = under[s, g]
+                m = face_moments([below_k[s](NORTH + j) for j in range(3)], n, lows[s, g])
+                r = rate(cur[s, g], k[s], tops[s, g], m, *cols[s, g])
+                if s == 0:
+                    x = [a + b for a, b in zip(cur[s, g], r)]
+                elif s == 1:
+                    x = [0.75 * a + 0.25 * (b + d) for a, b, d in zip(old[s, g], cur[s, g], r)]
+                else:
+                    sea = k[s](LAND)
+                    x = [sea * (THIRD * a + (2.0 * THIRD) * (b + d)) for a, b, d in zip(old[s, g], cur[s, g], r)]
+                done[s, g] = x, m, sth
+                if s + 1 < steps:
+                    under[s + 1, g] = row_traces(x)
+        for s in range(steps):
+            for g in both:
+                x, m, sth = done[s, g]
                 for j in range(3):
-                    fl[i, j] = m[j]
-                return n
-
-            if step == 0:
-                last = lax.fori_loop(0, 8, faces, tuple(ts[g, j] for j in range(3)))
-                w = [jnp.broadcast_to(kf[NORTH + j, 9:10, :], (8, COLS)) for j in range(3)]
-                m = face_moments(w, last, [tn[g, j] for j in range(3)])
-                for j in range(3):
-                    fl[8, j] = m[j]
-                rows = (0, 8)
-            else:
-                n, _ = row_traces([src[low, k] for k in range(6)])
-                lax.fori_loop(low + 1, high + 1, faces, n)
-                rows = (low + 1, high)
-
-            def update(i, _, src=src, step=step):
-                c = [src[i, k] for k in range(6)]
-
-                def k_of(j):
-                    return jnp.broadcast_to(kf[j, pl.ds(i + 2, 1), :], (8, COLS))
-
-                e, w = col_traces(c)
-                m = face_moments([k_of(EAST + j) for j in range(3)], e, [turn(x, -1, 1) for x in w])
-                p = 16 * i
-                em, wm = [], []
-                for j in range(3):
-                    rim = sx[step, j]
-                    at_east = pltpu.roll(rim, lax.rem(127 - 11 - p + 256, 128), 1)
-                    at_west = pltpu.roll(rim, lax.rem(256 - 3 - p, 128), 1)
-                    x = jnp.where(lane == COLS - 1, jnp.concatenate([at_east, at_east], 1), m[j])
-                    em.append(x)
-                    wm.append(jnp.where(lane == 0, jnp.concatenate([at_west, at_west], 1), turn(x, 1, 1)))
-                r = rate(c, k_of, [fl[i + 1, j] for j in range(3)], [fl[i, j] for j in range(3)], em, wm)
-                if step == 0:
-                    for k in range(6):
-                        c1[i, k] = c[k] + r[k]
-                elif step == 1:
-                    for k in range(6):
-                        c2[i, k] = 0.75 * c0[g, i, k] + 0.25 * (c[k] + r[k])
-                else:
-                    sea = k_of(LAND)
-                    for k in range(6):
-                        x = sea * (THIRD * c0[g, i, k] + (2.0 * THIRD) * (c[k] + r[k]))
+                    fl[s, g, j] = m[j]
+                    lo[s, g, j] = sth[j]
+                for j in range(6):
+                    if s < 2:
+                        (c1, c2)[s][w + s, g, j] = x[j]
+                    else:
                         for t in range(2):
-                            o_tr[pl.ds(g * 384 + k * 8 + t * 4 + i - 2, 8, stride=48), :] = x[:, t * 128:(t + 1) * 128]
-                return 0
-
-            lax.fori_loop(*rows, update, 0)
+                            o_tr[pl.ds(g * 384 + j * 8 + t * 4 + w, 8, stride=48), :] = x[j][:, t * 128:(t + 1) * 128]
+
+    def run(first_w, count, steps):
+        def body(i, _):
+            w = first_w - i
+            if steps == 3:
+                for n, at in enumerate((2, 1, 0)):
+                    pl.when(w == at)(functools.partial(arrive, [north_rows[n]]))
+            wave(w, steps)
+            return 0
+
+        lax.fori_loop(0, count, body, 0)
+
+    arrive(south_rows)
+    for g in both:
+        n, sth = row_traces(six(c0, 7, g))
+        open_face(0, 7, g, n, [tn[g, j] for j in range(3)], sth)
+    run(7, 2, 1)
+    for g in both:
+        n, sth = row_traces(six(c1, 6, g))
+        open_face(1, 6, g, n, row_traces(six(c1, 7, g))[1], sth)
+    run(5, 2, 2)
+    for g in both:
+        n, sth = row_traces(six(c2, 5, g))
+        open_face(2, 5, g, n, row_traces(six(c2, 6, g))[1], sth)
+    run(3, 4, 3)
 
     sent(first)
     sent(edges)
-    for some in bulk:
-        sent(some)
+    sent(north_rows)
+    sent(south_rows)
+
+
+def write_out(a, b, c, out_a, out_b, out_c, sem):
+    copies = [pltpu.make_async_copy(x, y, sem.at[i]) for i, (x, y) in enumerate(((a, out_a), (b, out_b), (c, out_c)))]
+    for copy in copies:
+        copy.start()
+    for copy in copies:
+        copy.wait()
 
 
 def local_step(nlat, nlon, tracers, velocity, stress, strength, inverse_mass, wind, ocean_mask):
     linear = tracers.reshape(NTR, 6, ROWS, 2, 128).transpose(0, 1, 3, 2, 4).reshape(768, 128)
     hbm = pl.BlockSpec(memory_space=pltpu.HBM)
     vmem = pl.BlockSpec(memory_space=pltpu.VMEM)
-    messages = 8 + 3 + 8 + 8
-    new_velocity, new_stress, new_tracers = pl.pallas_call(
+    messages = 8 + 3 + 8 + 6
+    shapes = ((2, ROWS, COLS), (3, ROWS, COLS), (768, 128))
+    given = [
+        pltpu.with_memory_space_constraint(x, pltpu.HBM)
+        for x in (linear, velocity, stress, strength, inverse_mass, wind, ocean_mask)
+    ]
+    results = pl.pallas_call(
         functools.partial(kernel, nlat, nlon),
-        out_shape=(
-            jax.ShapeDtypeStruct((2, ROWS, COLS), F32),
-            jax.ShapeDtypeStruct((3, ROWS, COLS), F32),
-            jax.ShapeDtypeStruct((768, 128), F32),
-        ),
+        out_shape=tuple(pltpu.VMEM(shape, F32) for shape in shapes),
         in_specs=[hbm] * 7,
         out_specs=(vmem, vmem, vmem),
         scratch_shapes=[
@@ -490,27 +535,35 @@
             pltpu.VMEM((2, 4, 2, 4, 128), F32),
             pltpu.VMEM((3, 8, 128), F32),
             pltpu.VMEM((8, 3, 8, 128), F32),
-            pltpu.VMEM((2, 8, 6, 8, COLS), F32),
+            pltpu.VMEM((8, 2, 6, 8, COLS), F32),
+            pltpu.VMEM((2, 2, 3, 8, COLS), F32),
             pltpu.VMEM((2, 3, 8, COLS), F32),
             pltpu.VMEM((2, 3, 8, COLS), F32),
             pltpu.VMEM((2, 3, 8, COLS), F32),
-            pltpu.VMEM((2, 3, 8, COLS), F32),
-            pltpu.VMEM((8, 6, 8, COLS), F32),
-            pltpu.VMEM((8, 6, 8, COLS), F32),
+            pltpu.VMEM((8, 2, 6, 8, COLS), F32),
+            pltpu.VMEM((8, 2, 6, 8, COLS), F32),
             pltpu.VMEM((COEFS, 16, COLS), F32),
             pltpu.VMEM((LAND, 8, 128), F32),
             pltpu.VMEM((12, 8, 128), F32),
-            pltpu.VMEM((6, 8, 128), F32),
-            pltpu.VMEM((3, 3, 8, 128), F32),
-            pltpu.VMEM((9, 3, 8, COLS), F32),
+            pltpu.VMEM((3, 2, 3, 8, 128), F32),
+            pltpu.VMEM((3, 2, 3, 8, COLS), F32),
+            pltpu.VMEM((3, 2, 3, 8, COLS), F32),
             pltpu.SemaphoreType.DMA((8,)),
             pltpu.SemaphoreType.DMA((messages,)),
             pltpu.SemaphoreType.DMA((messages,)),
         ],
         compiler_params=pltpu.CompilerParams(
-            collective_id=0, has_side_effects=True, vmem_limit_bytes=48 << 20
+            collective_id=0, has_side_effects=True, vmem_limit_bytes=16 << 20
         ),
-    )(linear, velocity, stress, strength, inverse_mass, wind, ocean_mask)
+    )(*given)
+    new_velocity, new_stress, new_tracers = pl.pallas_call(
+        write_out,
+        out_shape=tuple(jax.ShapeDtypeStruct(shape, F32) for shape in shapes),
+        in_specs=[vmem] * 3,
+        out_specs=(hbm, hbm, hbm),
+        scratch_shapes=[pltpu.SemaphoreType.DMA((3,))],
+        compiler_params=pltpu.CompilerParams(vmem_limit_bytes=16 << 20),
+    )(*results)
     new_tracers = new_tracers.reshape(NTR, 6, 2, ROWS, 128).transpose(0, 1, 3, 2, 4).reshape(NTR, 6, ROWS, COLS)
     return new_velocity, new_stress, new_tracers
 

time: 39.6 us -> 28.4 us (0.72)
  local copies, waits for them, and re-layouts: 7.09 us -> 0 us
  Pallas kernels: 31.5 us -> 27.6 us
    unnamed x17 -> x0, local copies, waits for them, and re-layouts: 7.09 us -> none
    pallas_call x1 -> x2, Pallas kernels: 31.5 us -> 27.6 us  [the longest x1 26.8 us: local_step(): pl.pallas_call(functools.partial(kernel, nlat, nlon), out_shape=tuple((pl...]
where the time goes in v2:
time: 28.4 us; the launch traced here: 28.2 us
  Pallas kernels  27.6 us (97%)
  between operations  0.64 us (2%)
    pallas_call x1, Pallas kernels, local_step(): pl.pallas_call(functools.partial(kernel, nlat, nlon), out_shape=tuple((pl...  26.8 us
    pallas_call x1, Pallas kernels, local_step(): pl.pallas_call(write_out, out_shape=tuple((jax.ShapeDtypeStruct(shape, F3...  0.78 us

profile of v2, /device:TPU:40, one launch (start us, length us, event | category | flops | bytes accessed | tf_op | source)
XLA Modules:
  0.0 28.2 jit_solution(6400723998241814309)
XLA Ops:
  0.6 26.8 %shard_map.94 = (f32[2,4,256]{2,1,0:T(4,128)S(1)}, f32[3,4,256]{2,1,0:T(4,128)S(1)}, f32[768,128]{1,0:T(8,128)S(1)}) custom-call(f32[768,128]{1,0:T(8,128)} %bitcast.10, f32[2,4,256]{2,1,0:T(4,128)} %vel.1, f32[3,4,256]{2,1,0:T(4,128)} %stress.1, f32[4,256]{1,0:T(4,128)} %strength.1, f32[4,256]{1,0:T(4,128)} %mass.1, f32[2,4,256]{2,1,0:T(4,128)} %wind.1, ...), custom_call_target="tpu_custom_call" | custom-call | tf_op jit(solution)/shard_map/pallas_call | solution.py:522
  27.4 0.8 %shard_map.95 = (f32[2,4,256]{2,1,0:T(4,128)}, f32[3,4,256]{2,1,0:T(4,128)}, f32[768,128]{1,0:T(8,128)}) custom-call(f32[2,4,256]{2,1,0:T(4,128)S(1)} %get-tuple-element.9.a, f32[3,4,256]{2,1,0:T(4,128)S(1)} %get-tuple-element.10.b, f32[768,128]{1,0:T(8,128)S(1)} %get-tuple-element.11.c), custom_call_target="tpu_custom_call" | custom-call | tf_op jit(solution)/shard_map/pallas_call | solution.py:559
